TPU v7x, 128 devices: a whole 4x4x4 slice. The times are simulated.
128 devices in a mesh: dp: 32 (over y, x, core), tensor: 4 (over z).
Axes of the slice: x: 4, y: 4, z: 4, core: 2. Of those that a mesh axis runs over, the one named last changes fastest.
Arguments:
- tokens: bfloat16 [77824, 768], P(('dp', 'tensor')), may hold values from -6 to 6
- prompt_table: float32 [100, 768], replicated, may hold values from -6 to 6
- lengths: int32 [256], P('dp'), may hold values from 1 to 100, as said below
- table_rows: int32 [256, 100], P('dp'), may hold values from 0 to 99
- ln1_gain: float32 [768], replicated, may hold values from 0.1 to 1.9
- ln1_bias: float32 [768], replicated, may hold values from -3 to 3
- w_qkv: float32 [3, 768, 768], P(None, 'dp', 'tensor'), may hold values from -0.21875 to 0.21875
- qv_bias: float32 [2, 768], P(None, 'tensor'), may hold values from -1.5 to 1.5
- w_out: float32 [768, 768], P('tensor', 'dp'), may hold values from -0.875 to 0.875
- out_bias: float32 [768], replicated, may hold values from -3 to 3
- ln2_gain: float32 [768], replicated, may hold values from 0.1 to 1.9
- ln2_bias: float32 [768], replicated, may hold values from -3 to 3
- w_up: float32 [768, 3072], P('dp', 'tensor'), may hold values from -0.21875 to 0.21875
- up_bias: float32 [3072], P('tensor'), may hold values from -3 to 3
- w_down: float32 [3072, 768], P('tensor', 'dp'), may hold values from -0.109375 to 0.109375
- down_bias: float32 [768], replicated, may hold values from -3 to 3
- cotangent: bfloat16 [77824, 768], P(('dp', 'tensor')), may hold values from -6 to 6
Outputs:
- output: bfloat16 [77824, 768], P(('dp', 'tensor'))
- token_grad: float32 [77824, 768], P(('dp', 'tensor'))
- table_grad: float32 [100, 768], replicated
Inputs may be any that keep to these rules, and one draw needn't show every extreme that they name: `lengths`: each image's prompt length is one of 1, 10, 50 and 100; in every draw some image has 100 and some has 1. `table_rows`: only the first lengths[i] slots of image i are used.
All inputs are finite; a program needn't handle non-finite values.
Results may differ from a plain program's by a relative error of at most 0.012.
The roundings to bfloat16 on the way count: a program that leaves them out, or rounds other values in their place, can miss the bound.
Values may be sent and summed in bfloat16 or wider, within the bound.
A program may use at most 128 MiB of HBM per device.

v0:
```python
import jax
import jax.numpy as jnp
from jax import lax
from jax.sharding import PartitionSpec as P

HD = 64
PATCHES = 197
PROMPTS = 100
SEQ = 304


EPSILON = 1e-06
MASKED_SCORE = -1e30
ROOT_HALF = 0.7071067811865476
GAUSS_DENSITY = 0.3989422804014327


def normalize(hidden_in):
    average = jnp.mean(hidden_in, axis=-1, keepdims=True)
    centered = hidden_in - average
    inv_scale = lax.rsqrt(jnp.mean(centered * centered, axis=-1, keepdims=True) + EPSILON)
    return (centered * inv_scale, inv_scale)


def norm_back(upstream, normed, inv_scale, norm_gain):
    scaled = upstream * norm_gain
    return inv_scale * (
        scaled
        - jnp.mean(scaled, axis=-1, keepdims=True)
        - normed * jnp.mean(scaled * normed, axis=-1, keepdims=True)
    )


def slot_layout(lengths, table_rows, first_row, row_count):
    places = first_row + jnp.arange(row_count, dtype=jnp.int32)
    image_ids = places // SEQ
    slot_ids = places - image_ids * SEQ
    matches = image_ids[:, None] == jnp.arange(lengths.shape[0], dtype=jnp.int32)[None, :]
    row_length = jnp.sum(jnp.where(matches, lengths[None, :], 0), axis=1)
    live_slot = (slot_ids >= PATCHES) & (slot_ids < PATCHES + row_length)
    flat_ids = image_ids * PROMPTS + jnp.clip(slot_ids - PATCHES, 0, PROMPTS - 1)
    picked = jnp.take(table_rows.reshape(-1), flat_ids)
    one_hot = (
        (picked[:, None] == jnp.arange(PROMPTS, dtype=jnp.int32)[None, :]) & live_slot[:, None]
    ).astype(jnp.float32)
    return (live_slot, one_hot)


def pair_scores(packed, key_live):
    queries = packed[:, :, 0]
    key_rows = packed[:, :, 1]
    factor = queries.shape[-1] ** (-0.5)
    scores = (
        jnp.einsum("pqhd,pkhd->phqk", queries, key_rows, preferred_element_type=jnp.float32)
        * factor
    )
    return (jnp.where(key_live[:, None, None, :], scores, MASKED_SCORE), factor)


def attend_pair(operands):
    packed, key_live = operands
    scores, factor = pair_scores(packed, key_live)
    highest = jnp.max(scores, axis=-1, keepdims=True)
    exponent = jnp.exp(scores - highest)
    row_total = jnp.sum(exponent, axis=-1, keepdims=True)
    probs_low = (exponent / row_total).astype(jnp.bfloat16)
    attended = jnp.einsum(
        "phqk,pkhd->pqhd", probs_low, packed[:, :, 2], preferred_element_type=jnp.float32
    )
    return (attended.astype(jnp.bfloat16), highest + jnp.log(row_total))


def attend_back(operands):
    packed, key_live, log_total, d_attended = operands
    scores, factor = pair_scores(packed, key_live)
    probs = jnp.exp(scores - log_total)
    probs_low = probs.astype(jnp.bfloat16)
    d_probs = jnp.einsum(
        "pqhd,pkhd->phqk", d_attended, packed[:, :, 2], preferred_element_type=jnp.float32
    )
    d_values = jnp.einsum(
        "phqk,pqhd->pkhd", probs_low, d_attended, preferred_element_type=jnp.float32
    )
    d_scores = (probs * (d_probs - jnp.sum(d_probs * probs, axis=-1, keepdims=True))).astype(
        jnp.bfloat16
    )
    d_queries = (
        jnp.einsum("phqk,pkhd->pqhd", d_scores, packed[:, :, 1], preferred_element_type=jnp.float32)
        * factor
    )
    d_keys = (
        jnp.einsum("phqk,pqhd->pkhd", d_scores, packed[:, :, 0], preferred_element_type=jnp.float32)
        * factor
    )
    return jnp.stack([d_queries, d_keys, d_values], axis=2).astype(jnp.bfloat16)


def body(
    tokens,
    prompt_table,
    lengths,
    table_rows,
    ln1_gain,
    ln1_bias,
    w_qkv,
    qv_bias,
    w_out,
    out_bias,
    ln2_gain,
    ln2_bias,
    w_up,
    up_bias,
    w_down,
    down_bias,
    cotangent,
):
    row_count = tokens.shape[0]
    first_row = lax.axis_index("tensor") * row_count
    group_rows = row_count * lax.axis_size("tensor")
    image_count = lengths.shape[0]
    pair_count = image_count // 2
    live_slot, one_hot = slot_layout(lengths, table_rows, first_row, row_count)
    slot_ids = jnp.arange(SEQ, dtype=jnp.int32)
    key_live = slot_ids[None, :] < PATCHES + lengths[:, None]
    mask_pairs = key_live.reshape(pair_count, 2, SEQ)
    qkv_w, out_w, up_w, down_w = (
        lax.all_gather(w_qkv.astype(jnp.bfloat16), "dp", axis=1, tiled=True),
        lax.all_gather(w_out.astype(jnp.bfloat16), "dp", axis=1, tiled=True),
        lax.all_gather(w_up.astype(jnp.bfloat16), "dp", axis=0, tiled=True),
        lax.all_gather(w_down.astype(jnp.bfloat16), "dp", axis=1, tiled=True),
    )
    local_width = qkv_w.shape[2]
    heads_here = local_width // HD
    prompt_rows = jnp.dot(one_hot, prompt_table, precision=lax.Precision.HIGHEST)
    inputs = jnp.where(live_slot[:, None], prompt_rows, tokens.astype(jnp.float32))
    first_normed, first_scale = normalize(inputs)
    first_in = (first_normed * ln1_gain + ln1_bias).astype(jnp.bfloat16)
    projected = jnp.einsum(
        "rd,cdk->rck",
        lax.all_gather(first_in, "tensor", axis=0, tiled=True),
        qkv_w,
        preferred_element_type=jnp.float32,
    )
    bias_rows = jnp.stack([qv_bias[0], jnp.zeros_like(qv_bias[0]), qv_bias[1]])
    qkv_low = (projected + bias_rows).astype(jnp.bfloat16)
    packed = qkv_low.reshape(pair_count, 2, SEQ, 3, heads_here, HD)
    attended, log_total = lax.map(attend_pair, (packed, mask_pairs))
    attended = attended.reshape(group_rows, local_width)
    branch_sum = lax.psum_scatter(
        jnp.dot(attended, out_w, preferred_element_type=jnp.float32),
        "tensor",
        scatter_dimension=0,
        tiled=True,
    )
    middle = inputs + branch_sum + out_bias
    second_normed, second_scale = normalize(middle)
    second_in = (second_normed * ln2_gain + ln2_bias).astype(jnp.bfloat16)
    upper = jnp.dot(
        lax.all_gather(second_in, "tensor", axis=0, tiled=True),
        up_w,
        preferred_element_type=jnp.float32,
    )
    upper = upper + up_bias
    hidden = jax.nn.gelu(upper, approximate=False).astype(jnp.bfloat16)
    mixed = lax.psum_scatter(
        jnp.dot(hidden, down_w, preferred_element_type=jnp.float32),
        "tensor",
        scatter_dimension=0,
        tiled=True,
    )
    output = (middle + mixed + down_bias).astype(jnp.bfloat16)
    qkv_w, out_w, up_w, down_w = (
        lax.all_gather(w_qkv.astype(jnp.bfloat16), "dp", axis=1, tiled=True),
        lax.all_gather(w_out.astype(jnp.bfloat16), "dp", axis=1, tiled=True),
        lax.all_gather(w_up.astype(jnp.bfloat16), "dp", axis=0, tiled=True),
        lax.all_gather(w_down.astype(jnp.bfloat16), "dp", axis=1, tiled=True),
    )
    d_hidden = jnp.einsum(
        "rd,fd->rf",
        lax.all_gather(cotangent, "tensor", axis=0, tiled=True),
        down_w,
        preferred_element_type=jnp.float32,
    )
    normal_cdf = 0.5 * (1.0 + lax.erf(upper * ROOT_HALF))
    gelu_slope = normal_cdf + upper * GAUSS_DENSITY * jnp.exp(-0.5 * upper * upper)
    d_upper = (d_hidden * gelu_slope).astype(jnp.bfloat16)
    d_second = lax.psum_scatter(
        jnp.einsum("rf,df->rd", d_upper, up_w, preferred_element_type=jnp.float32),
        "tensor",
        scatter_dimension=0,
        tiled=True,
    )
    d_middle = cotangent.astype(jnp.float32) + norm_back(
        d_second, second_normed, second_scale, ln2_gain
    )
    d_middle_low = d_middle.astype(jnp.bfloat16)
    d_attended = jnp.einsum(
        "rd,kd->rk",
        lax.all_gather(d_middle_low, "tensor", axis=0, tiled=True),
        out_w,
        preferred_element_type=jnp.float32,
    ).astype(jnp.bfloat16)
    d_pairs = d_attended.reshape(pair_count, 2, SEQ, heads_here, HD)
    d_qkv = lax.map(attend_back, (packed, mask_pairs, log_total, d_pairs))
    d_qkv = d_qkv.reshape(group_rows, 3, local_width)
    d_first = lax.psum_scatter(
        jnp.einsum("rck,cdk->rd", d_qkv, qkv_w, preferred_element_type=jnp.float32),
        "tensor",
        scatter_dimension=0,
        tiled=True,
    )
    d_inputs = d_middle + norm_back(d_first, first_normed, first_scale, ln1_gain)
    token_grad = jnp.where(live_slot[:, None], 0.0, d_inputs)
    local_table = jnp.einsum("rp,rd->pd", one_hot, d_inputs, precision=lax.Precision.HIGHEST)
    table_grad = lax.psum(local_table, ("dp", "tensor"))
    return (output, token_grad, table_grad)


def solution(mesh):
    return jax.shard_map(
        body,
        mesh=mesh,
        in_specs=(
            P(("dp", "tensor"), None),
            P(),
            P("dp"),
            P("dp", None),
            P(),
            P(),
            P(None, "dp", "tensor"),
            P(None, "tensor"),
            P("tensor", "dp"),
            P(),
            P(),
            P(),
            P("dp", "tensor"),
            P("tensor"),
            P("tensor", "dp"),
            P(),
            P(("dp", "tensor"), None),
        ),
        out_specs=(P(("dp", "tensor"), None), P(("dp", "tensor"), None), P()),
        check_vma=False,
    )
```

profile of v0, /device:TPU:1, one launch (start us, length us, event | category | flops | bytes accessed | tf_op | source)
XLA Modules:
  0.0 827.1 jit_solution(18058036637845431058)
XLA Ops:
  9.0 2.8 gather_fusion
  12.0 1.2 fusion.90
  13.6 1.3 add_convert_fusion.3
  15.2 26.5 %all_gather.30 = bf16[192,768]{0,1:T(8,128)(2,1)S(1)} all-gather(bf16[192,24]{0,1:T(8,128)(2,1)S(1)} %convert_element_type.74), channel_id=1, replica_groups=mesh['dp'=32,'tensor'=4] {'dp'}, dimensions={1}, use_global_device_ids=true | all-gather | bytes 304128 | tf_op jit(solution)/shard_map/all_gather | solution.py:128
  41.7 27.0 %all_gather.29 = bf16[3,768,192]{2,1,0:T(8,128)(2,1)} all-gather(bf16[3,24,192]{2,1,0:T(8,128)(2,1)S(1)} %convert_element_type.72), channel_id=1, replica_groups=mesh['dp'=32,'tensor'=4] {'dp'}, dimensions={1}, use_global_device_ids=true | all-gather | bytes 912384 | tf_op jit(solution)/shard_map/all_gather | solution.py:127
  68.9 6.5 add_convert_fusion
  75.3 7.4 reshape.239
  82.8 4.5 copy.40
  87.3 21.5 %while.22 = (s32[]{:T(128)}, bf16[4,2,304,3,64]{2,1,0,4,3:T(2,128)(2,1)}, f32[4,2,3,304,1]{3,2,1,4,0:T(4,128)}, bf16[4,2,304,3,3,64]{2,5,4,1,3,0:T(8,128)(2,1)}, pred[4,2,304]{2,1,0:T(4,128)(4,1)S(1)}, /*index=5*/s32[]{:T(128)}) while((s32[]{:T(128)}, bf16[4,2,304,3,64]{2,1,0,4,3:T(2,128)(2,1)}, f32[4,2,3,304,1]{3,2,1,4,0:T(4,128)}, ...), condition=%wide.region_6.7_spmd, body=%wide.region_3.6_spmd.sunk | while | flops 148719840 | bytes 10364397 | solution.py:147
  87.3 1.3 dynamic-slice_bitcast_fusion.11
  92.7 1.3 dynamic-slice_bitcast_fusion.11
  98.1 1.3 dynamic-slice_bitcast_fusion.11
  103.4 1.3 dynamic-slice_bitcast_fusion.11
  108.8 2.0 reshape.240
  110.8 4.2 fusion.91
  116.7 71.4 %reduce-scatter.5.cloned.1.call-done = f32[608,768]{1,0:T(8,128)} async-done(((f32[2432,768]{1,0:T(8,128)}), f32[608,768]{1,0:T(8,128)}) %reduce-scatter.5.cloned.1.call-update) | async-done | bytes 1867792 | tf_op jit(solution)/shard_map/reduce_scatter | solution.py:149
  188.1 1.9 fusion.88
  191.2 1.3 add_convert_fusion.2
  194.3 42.3 %all-gather.9.cloned.1.call-done = bf16[2432,768]{1,0:T(8,128)(2,1)} async-done(((bf16[608,768]{1,0:T(8,128)(2,1)}), bf16[2432,768]{1,0:T(8,128)(2,1)}) %all-gather.9.cloned.1.call-update) | async-done | bytes 3735568 | tf_op jit(solution)/shard_map/all_gather | solution.py:159
  236.6 8.4 %fusion.92 = f32[2432,768]{1,0:T(8,128)} fusion(bf16[2432,768]{1,0:T(8,128)(2,1)} %all-gather.9.cloned.1.call-done, bf16[768,768]{1,0:T(8,128)(2,1)} %all-gather.11.cloned.1.call-done), kind=kOutput, calls=%fused_computation.165 | convolution fusion | flops 2868903936 | bytes 12386304 | tf_op jit(solution)/shard_map/dot_general | solution.py:158
  245.0 37.3 %all-gather.13.cloned.1.call-done = bf16[768,768]{0,1:T(8,128)(2,1)} async-done(((bf16[768,24]{0,1:T(8,128)(2,1)}), bf16[768,768]{0,1:T(8,128)(2,1)}) %all-gather.13.cloned.1.call-update) | async-done | bytes 1179664 | tf_op jit(solution)/shard_map/all_gather | solution.py:130
  282.3 45.1 %all-gather.15.cloned.1.call-done = bf16[2432,768]{1,0:T(8,128)(2,1)} async-done(((bf16[608,768]{1,0:T(8,128)(2,1)}), bf16[2432,768]{1,0:T(8,128)(2,1)}) %all-gather.15.cloned.1.call-update) | async-done | bytes 3735568 | tf_op jit(solution)/shard_map/all_gather | solution.py:180
  327.4 13.0 %fusion.39 = f32[2432,768]{1,0:T(8,128)} fusion(bf16[768,768]{1,0:T(8,128)(2,1)} %all-gather.11.cloned.1.call-done, f32[2432,768]{1,0:T(8,128)} %fusion.92, bf16[2432,768]{1,0:T(8,128)(2,1)} %all-gather.15.cloned.1.call-done, bf16[768,768]{0,1:T(8,128)(2,1)} %all-gather.13.cloned.1.call-done, f32[768]{0:T(1024)S(1)} %copy-done.29), kind=kOutput, calls=%fused_computation.88 | convolution fusion | flops 5758353408 | bytes 21040128 | tf_op jit(solution)/shard_map/rf,df->rd/dot_general | solution.py:188
  340.5 21.6 %fusion.37 = f32[2432,768]{1,0:T(8,128)} fusion(bf16[768,768]{0,1:T(8,128)(2,1)} %all-gather.13.cloned.1.call-done, f32[2432,768]{1,0:T(8,128)} %fusion.92, f32[768]{0:T(1024)S(1)} %copy-done.29), kind=kOutput, calls=%fused_computation.72 | convolution fusion | flops 2992177152 | bytes 16124928 | tf_op jit(solution)/shard_map/dot_general | solution.py:166
  362.1 52.3 %reduce-scatter.9.cloned.1.call-done = f32[608,768]{1,0:T(8,128)} async-done(((f32[2432,768]{1,0:T(8,128)}), f32[608,768]{1,0:T(8,128)}) %reduce-scatter.9.cloned.1.call-update) | async-done | bytes 1867792 | tf_op jit(solution)/shard_map/reduce_scatter | solution.py:187
  414.4 2.7 multiply_reduce_fusion.6
  417.1 73.1 %reduce-scatter.7.cloned.1.call-done = f32[608,768]{1,0:T(8,128)} async-done(((f32[2432,768]{1,0:T(8,128)}), f32[608,768]{1,0:T(8,128)}) %reduce-scatter.7.cloned.1.call-update) | async-done | bytes 1867792 | tf_op jit(solution)/shard_map/reduce_scatter | solution.py:165
  490.2 4.3 fusion.87
  494.8 44.2 %all-gather.17.cloned.1.call-done = bf16[2432,768]{1,0:T(8,128)(2,1)} async-done(((bf16[608,768]{1,0:T(8,128)(2,1)}), bf16[2432,768]{1,0:T(8,128)(2,1)}) %all-gather.17.cloned.1.call-update) | async-done | bytes 3735568 | tf_op jit(solution)/shard_map/all_gather | solution.py:199
  539.0 3.4 convolution_convert_fusion
  542.4 2.4 reshape.241
  544.8 35.0 %while.23 = (s32[]{:T(128)}, bf16[4,2,304,3,3,64]{2,1,0,5,4,3:T(2,128)(2,1)}, bf16[4,2,304,3,3,64]{2,5,4,1,3,0:T(8,128)(2,1)}, pred[4,2,304]{2,1,0:T(4,128)(4,1)...) while((s32[]{:T(128)}, ...), condition=%wide.region_16.17_spmd, body=%wide.region_14.16_spmd.sunk | while | flops 361150176 | bytes 25404188 | solution.py:204
  544.8 1.3 dynamic-slice_bitcast_fusion.14
  551.6 1.9 copy_dynamic-update-slice_fusion.5
  553.5 1.3 dynamic-slice_bitcast_fusion.14
  560.3 1.9 copy_dynamic-update-slice_fusion.5
  562.2 1.3 dynamic-slice_bitcast_fusion.14
  569.1 1.9 copy_dynamic-update-slice_fusion.5
  571.0 1.3 dynamic-slice_bitcast_fusion.14
  577.9 1.9 copy_dynamic-update-slice_fusion.5
  579.8 6.5 reshape.242
  586.3 8.0 convolution_bitcast_fusion
  594.4 74.1 %reduce-scatter.11.cloned.1.call-done = f32[608,768]{1,0:T(8,128)} async-done(((f32[2432,768]{1,0:T(8,128)}), f32[608,768]{1,0:T(8,128)}) %reduce-scatter.11.cloned.1.call-update) | async-done | bytes 1867792 | tf_op jit(solution)/shard_map/reduce_scatter | solution.py:206
  668.5 2.3 multiply_reduce_fusion.5
  671.1 1.8 broadcast_select_fusion
  672.9 1.7 fusion.41
  674.7 143.1 %all-reduce.2.cloned.1.call-done = f32[100,768]{1,0:T(8,128)} async-done(((f32[100,768]{1,0:T(8,128)}), f32[100,768]{1,0:T(8,128)}) %all-reduce.2.cloned.1.call-update) | async-done | bytes 307216 | tf_op jit(solution)/shard_map/psum | solution.py:215
  817.8 1.7 copy.90
  (177 shorter events, 45.8 us)
Async XLA Ops:
  8.0 4.0 copy-start
  8.0 3.8 copy-start.28
  8.0 4.0 copy-start.7
  8.0 60.8 %all-gather.7.cloned.1.call-start = ((), (), s32[]{:S(2)}) async-start(), calls=%async_computation.4 | async-start | bytes 4669440 | tf_op jit(solution)/shard_map/all_gather | solution.py:140
  11.8 1.8 copy-start.18
  11.8 1.8 copy-start.23
  11.8 1.4 copy-start.15
  12.0 1.6 copy-start.21
  13.2 1.8 copy-start.8
  13.2 1.8 copy-start.10
  13.2 1.9 copy-start.20
  13.6 55.1 %copy-start.27 = (f32[2,192]{1,0:T(2,128)S(1)}, f32[2,192]{1,0:T(2,128)}, u32[]{:S(2)}) copy-start(f32[2,192]{1,0:T(2,128)} %param.28) | copy-start | bytes 4612
  13.6 1.4 copy-start.13
  15.0 173.1 %reduce-scatter.5.cloned.1.call-start = ((), (), s32[]{:S(2)}) async-start(), calls=%async_computation.5 | async-start | bytes 9338880 | tf_op jit(solution)/shard_map/reduce_scatter | solution.py:149
  115.1 0.9 copy-start.11
  115.1 73.0 %copy-start.26 = (f32[768]{0:T(1024)S(1)}, f32[768]{0:T(1024)}, u32[]{:S(2)}) copy-start(f32[768]{0:T(1024)} %param.30) | copy-start | bytes 9220
  115.1 79.2 %all-gather.11.cloned.1.call-start = ((), (), s32[]{:S(2)}) async-start(), calls=%async_computation.7 | async-start | bytes 1216512 | tf_op jit(solution)/shard_map/all_gather | solution.py:129
  116.6 74.7 %copy-start.17 = (f32[768]{0:T(1024)S(1)}, f32[768]{0:T(1024)}, u32[]{:S(2)}) copy-start(f32[768]{0:T(1024)} %param.31) | copy-start | bytes 9220
  116.6 74.6 %copy-start.24 = (f32[768]{0:T(1024)S(1)}, f32[768]{0:T(1024)}, u32[]{:S(2)}) copy-start(f32[768]{0:T(1024)} %param.32) | copy-start | bytes 9220
  116.6 120.0 %all-gather.9.cloned.1.call-start = ((), (), s32[]{:S(2)}) async-start(), calls=%async_computation.6 | async-start | bytes 4669440 | tf_op jit(solution)/shard_map/all_gather | solution.py:159
  190.0 1.2 copy-start.2
  190.0 2.6 copy-start.12
  192.5 89.8 %all-gather.13.cloned.1.call-start = ((), (), s32[]{:S(2)}) async-start(), calls=%async_computation.8 | async-start | bytes 1216512 | tf_op jit(solution)/shard_map/all_gather | solution.py:130
  193.2 134.2 %all-gather.15.cloned.1.call-start = ((), (), s32[]{:S(2)}) async-start(), calls=%async_computation.10 | async-start | bytes 4669440 | tf_op jit(solution)/shard_map/all_gather | solution.py:180
  194.0 133.4 %copy-start.29 = (f32[768]{0:T(1024)S(1)}, f32[768]{0:T(1024)}, u32[]{:S(2)}) copy-start(f32[768]{0:T(1024)} %param.34) | copy-start | bytes 9220
  194.0 220.4 %reduce-scatter.9.cloned.1.call-start = ((), (), s32[]{:S(2)}) async-start(), calls=%async_computation.11 | async-start | bytes 9338880 | tf_op jit(solution)/shard_map/reduce_scatter | solution.py:187
  340.4 149.7 %reduce-scatter.7.cloned.1.call-start = ((), (), s32[]{:S(2)}) async-start(), calls=%async_computation.9 | async-start | bytes 9338880 | tf_op jit(solution)/shard_map/reduce_scatter | solution.py:165
  362.1 128.1 %copy-start.5 = (bf16[608,768]{1,0:T(8,128)(2,1)S(1)}, bf16[608,768]{1,0:T(8,128)(2,1)}, u32[]{:S(2)}) copy-start(bf16[608,768]{1,0:T(8,128)(2,1)} %param.37) | copy-start | bytes 2801668
  362.1 128.1 %copy-start.25 = (f32[768]{0:T(1024)S(1)}, f32[768]{0:T(1024)}, u32[]{:S(2)}) copy-start(f32[768]{0:T(1024)} %param.36) | copy-start | bytes 9220
  362.1 176.9 %all-gather.17.cloned.1.call-start = ((), (), s32[]{:S(2)}) async-start(), calls=%async_computation.12 | async-start | bytes 4669440 | tf_op jit(solution)/shard_map/all_gather | solution.py:199
  494.5 174.0 %reduce-scatter.11.cloned.1.call-start = ((), (), s32[]{:S(2)}) async-start(), calls=%async_computation.13 | async-start | bytes 9338880 | tf_op jit(solution)/shard_map/reduce_scatter | solution.py:206
  579.8 6.5 copy-start.6
  594.3 74.2 %copy-start.9 = (f32[608]{0:T(1024)S(1)}, f32[608]{0:T(1024)}, u32[]{:S(2)}) copy-start(f32[608]{0:T(1024)} %copy-done.8) | copy-start | bytes 7300
  594.3 74.2 %copy-start.14 = (f32[608]{0:T(1024)S(1)}, f32[608]{0:T(1024)}, u32[]{:S(2)}) copy-start(f32[608]{0:T(1024)} %copy-done.13) | copy-start | bytes 7300
  594.3 74.2 %copy-start.19 = (f32[768]{0:T(1024)S(1)}, f32[768]{0:T(1024)}, u32[]{:S(2)}) copy-start(f32[768]{0:T(1024)} %param.25) | copy-start | bytes 9220
  594.3 76.5 %copy-start.22 = (pred[608]{0:T(1024)(128)(4,1)S(1)}, pred[608]{0:T(1024)(128)(4,1)}, u32[]{:S(2)}) copy-start(pred[608]{0:T(1024)(128)(4,1)} %copy-done.21) | copy-start | bytes 1828
  594.4 223.4 %all-reduce.2.cloned.1.call-start = ((), (), s32[]{:S(2)}) async-start(), calls=%async_computation.14 | async-start | bytes 638976 | tf_op jit(solution)/shard_map/psum | solution.py:215
  668.5 2.4 copy-start.3
  668.5 2.6 copy-start.4
  671.1 1.8 copy-start.16
  671.1 148.4 %copy-start.1 = (f32[100,768]{1,0:T(8,128)S(1)}, f32[100,768]{1,0:T(8,128)}, u32[]{:S(2)}) copy-start(f32[100,768]{1,0:T(8,128)} %param.22) | copy-start | bytes 921604
Sparse Core Ops, SparseCore 0:
  15.1 47.8 all-gather.6
  115.2 72.8 reduce-scatter.4
  494.6 44.3 all-gather.16
  594.5 73.9 reduce-scatter.10
  674.8 142.9 all-reduce.1
Sparse Core Ops, SparseCore 1:
  117.9 42.2 all-gather.10
  192.6 43.9 all-gather.8
  238.8 43.5 all-gather.12
  284.0 43.3 all-gather.14
  340.5 73.9 reduce-scatter.8
  416.9 73.2 reduce-scatter.6
where the time goes:
time: 832 us; the launch traced here: 827 us
  waiting for transfers between devices  584 us (70%)
  matrix products  87.3 us (10%)
  local copies, waits for them, and re-layouts  59.9 us (7%)
  blocking collectives  53.4 us (6%)
  other arithmetic  25.4 us (3%)
  between operations  16.2 us (2%)
    psum x1, waiting for transfers between devices, body(): table_grad = lax.psum(local_table, ('dp', 'tensor'))  143 us
    reduce_scatter x1, waiting for transfers between devices, body(): lax.psum_scatter(jnp.einsum('rck,cdk->rd', d_qkv, qkv_w, preferred_elemen...  74.1 us
    reduce_scatter x1, waiting for transfers between devices, body(): lax.psum_scatter(jnp.dot(hidden, down_w, preferred_element_type=jnp.float...  73.1 us
    reduce_scatter x1, waiting for transfers between devices, body(): lax.psum_scatter(jnp.dot(attended, out_w, preferred_element_type=jnp.floa...  71.4 us
    reduce_scatter x1, waiting for transfers between devices, body(): lax.psum_scatter(jnp.einsum('rf,df->rd', d_upper, up_w, preferred_element...  52.3 us
    all_gather x1, waiting for transfers between devices, body(): lax.all_gather(cotangent, 'tensor', axis=0, tiled=True)  45.1 us
    all_gather x1, waiting for transfers between devices, body(): lax.all_gather(d_middle_low, 'tensor', axis=0, tiled=True)  44.2 us
    all_gather x1, waiting for transfers between devices, body(): lax.all_gather(second_in, 'tensor', axis=0, tiled=True)  42.3 us
  transfers between devices with their start and end apart: 11, of which 9 were waited for; matrix products, arithmetic and copies ran while one was open for 5% of the time, Pallas kernels for 0%

commit v1 on v0

v1 whole, which is shorter than its diff:
```python
import functools
import jax
import jax.numpy as jnp
from jax import lax
from jax.experimental import pallas as pl
from jax.experimental.pallas import tpu as pltpu
from jax.sharding import PartitionSpec as P

D = 768
HD = 64
PATCHES = 197
PROMPTS = 100
SEQ = 304
NZ = 4
HZ = 3
QW = 192
FZ = 768
EPSILON = 1e-06
MASKED = -1e30
F32 = jnp.float32
BF = jnp.bfloat16
NN = (((1,), (0,)), ((), ()))
NT = (((1,), (1,)), ((), ()))
TN = (((0,), (0,)), ((), ()))
CH = 32


def mm(a, b, dims=NN):
    return lax.dot_general(a, b, dims, preferred_element_type=F32)


def gelu_pair(u):
    a = jnp.abs(u)
    t = 1.0 / (1.0 + (0.3275911 * 0.7071067811865476) * a)
    e = jnp.exp(-0.5 * (u * u))
    poly = t * (0.254829592 + t * (-0.284496736 + t * (1.421413741 + t * (-1.453152027 + t * 1.061405429))))
    half = 0.5 * poly * e
    cdf = jnp.where(u >= 0, 1.0 - half, half)
    return u * cdf, cdf + u * (0.3989422804014327 * e)


def stats(h):
    mean = jnp.mean(h, axis=-1, keepdims=True)
    c = h - mean
    r = lax.rsqrt(jnp.mean(c * c, axis=-1, keepdims=True) + EPSILON)
    return c * r, r


def norm_back(g, n, r, gain):
    e = g * gain
    return r * (e - jnp.mean(e, axis=-1, keepdims=True) - n * jnp.mean(e * n, axis=-1, keepdims=True))


def compute(rows, lens, tok, table, trows, g1, b1, qvb, ob, g2, b2, upb, db, cot,
            wqkv, wout, wup, wdn, out, tgrad, pgrad,
            inp, fin, qkv, probs, att, mid, sin, hid, dup, dmid, dml, dat, dqkv):
    t = lax.axis_index("tensor")
    images = rows // SEQ
    hots = []
    for i in range(images):
        base = jnp.concatenate([trows[pl.ds(t * images + i, 1), :], jnp.full((1, 384 - PROMPTS), -1, jnp.int32)], axis=1)
        slot = pltpu.roll(base, PATCHES, 1)
        slot = slot[:, :SEQ]
        place = lax.broadcasted_iota(jnp.int32, (1, SEQ), 1)
        live = (place >= PATCHES) & (place < PATCHES + lens[t * images + i])
        slot = jnp.where(live, slot, -1)
        prow = lax.broadcasted_iota(jnp.int32, (PROMPTS, SEQ), 0)
        hots.append((prow == slot).astype(F32))
    for i in range(images):
        place = lax.broadcasted_iota(jnp.int32, (SEQ, 1), 0)
        live = (place >= PATCHES) & (place < PATCHES + lens[t * images + i])
        picked = lax.dot_general(hots[i], table[...], TN, precision=lax.Precision.HIGHEST, preferred_element_type=F32)
        inp[pl.ds(i * SEQ, SEQ), :] = jnp.where(live, picked, tok[pl.ds(i * SEQ, SEQ), :].astype(F32))

    @pl.loop(0, rows // CH)
    def _(c):
        sl = pl.ds(pl.multiple_of(c * CH, CH), CH)
        n, _ = stats(inp[sl, :])
        fin[sl, :] = (n * g1[...] + b1[...]).astype(BF)

    @pl.loop(0, NZ)
    def _(z):
        x = mm(fin[...], wqkv[z])
        qkv[z] = (x + qvb[z]).astype(BF)

    @pl.loop(0, NZ)
    def _(z):
        for i in range(images):
            rs = pl.ds(i * SEQ, SEQ)
            blk = qkv[z, rs, :]
            place = lax.broadcasted_iota(jnp.int32, (1, SEQ), 1)
            bias = jnp.where(place < PATCHES + lens[t * images + i], 0.0, MASKED)
            outs = []
            for h in range(HZ):
                q = blk[:, h * HD:(h + 1) * HD] * 0.125
                k = blk[:, QW + h * HD:QW + (h + 1) * HD]
                v = blk[:, 2 * QW + h * HD:2 * QW + (h + 1) * HD]
                s = mm(q.astype(BF), k, NT) + bias
                m = jnp.max(s, axis=-1, keepdims=True)
                e = jnp.exp(s - m)
                p = (e / jnp.sum(e, axis=-1, keepdims=True)).astype(BF)
                probs[z, i * HZ + h] = p
                outs.append(mm(p, v).astype(BF))
            att[z, rs, :] = jnp.concatenate(outs, axis=1)

    @pl.loop(0, images)
    def _(i):
        rs = pl.ds(pl.multiple_of(i * SEQ, SEQ), SEQ)
        acc = mm(att[0, rs, :], wout[0], NT)
        for z in range(1, NZ):
            acc += mm(att[z, rs, :], wout[z], NT)
        mid[rs, :] = inp[rs, :] + acc + ob[...]

    @pl.loop(0, rows // CH)
    def _(c):
        sl = pl.ds(pl.multiple_of(c * CH, CH), CH)
        n, _ = stats(mid[sl, :])
        sin[sl, :] = (n * g2[...] + b2[...]).astype(BF)

    TF = 256
    NF = FZ // TF

    @pl.loop(0, NZ * NF)
    def _(j):
        z = j // NF
        f = pl.ds(pl.multiple_of((j % NF) * TF, TF), TF)
        fo = pl.ds(pl.multiple_of(j * TF, TF), TF)
        for i in range(images):
            rs = pl.ds(i * SEQ, SEQ)
            u = mm(sin[rs, :], wup[z, :, f]) + upb[z, :, f]
            dh = mm(cot[rs, :], wdn[z, :, f])
            a, b = gelu_pair(u)
            hid[rs, fo] = a.astype(BF)
            dup[rs, fo] = (dh * b).astype(BF)

    @pl.loop(0, images)
    def _(i):
        rs = pl.ds(pl.multiple_of(i * SEQ, SEQ), SEQ)
        acc = mm(hid[rs, 0:FZ], wdn[0], NT)
        for z in range(1, NZ):
            acc += mm(hid[rs, z * FZ:(z + 1) * FZ], wdn[z], NT)
        out[rs, :] = (mid[rs, :] + acc + db[...]).astype(BF)

    @pl.loop(0, images)
    def _(i):
        rs = pl.ds(pl.multiple_of(i * SEQ, SEQ), SEQ)
        acc = mm(dup[rs, 0:FZ], wup[0], NT)
        for z in range(1, NZ):
            acc += mm(dup[rs, z * FZ:(z + 1) * FZ], wup[z], NT)
        dmid[rs, :] = acc

    @pl.loop(0, rows // CH)
    def _(c):
        sl = pl.ds(pl.multiple_of(c * CH, CH), CH)
        n, r = stats(mid[sl, :])
        d = cot[sl, :].astype(F32) + norm_back(dmid[sl, :], n, r, g2[...])
        dmid[sl, :] = d
        dml[sl, :] = d.astype(BF)

    @pl.loop(0, NZ)
    def _(z):
        dat[z] = mm(dml[...], wout[z]).astype(BF)

    @pl.loop(0, NZ)
    def _(z):
        for i in range(images):
            rs = pl.ds(i * SEQ, SEQ)
            blk = qkv[z, rs, :]
            db_ = dat[z, rs, :]
            dq, dk, dv = [], [], []
            for h in range(HZ):
                q = blk[:, h * HD:(h + 1) * HD]
                k = blk[:, QW + h * HD:QW + (h + 1) * HD]
                v = blk[:, 2 * QW + h * HD:2 * QW + (h + 1) * HD]
                do = db_[:, h * HD:(h + 1) * HD]
                p = probs[z, i * HZ + h]
                dp = mm(do, v, NT)
                dv.append(mm(p, do, TN).astype(BF))
                pf = p.astype(F32)
                x = dp * pf
                ds = (x - pf * jnp.sum(x, axis=-1, keepdims=True)).astype(BF)
                dq.append((mm(ds, k) * 0.125).astype(BF))
                dk.append((mm(ds, q, TN) * 0.125).astype(BF))
            dqkv[z, rs, :] = jnp.concatenate(dq + dk + dv, axis=1)

    @pl.loop(0, images)
    def _(i):
        rs = pl.ds(pl.multiple_of(i * SEQ, SEQ), SEQ)
        acc = mm(dqkv[0, rs, :], wqkv[0], NT)
        for z in range(1, NZ):
            acc += mm(dqkv[z, rs, :], wqkv[z], NT)
        tgrad[rs, :] = acc

    @pl.loop(0, rows // CH)
    def _(c):
        sl = pl.ds(pl.multiple_of(c * CH, CH), CH)
        n, r = stats(inp[sl, :])
        d = dmid[sl, :] + norm_back(tgrad[sl, :], n, r, g1[...])
        tgrad[sl, :] = d

    total = None
    for i in range(images):
        rs = pl.ds(i * SEQ, SEQ)
        place = lax.broadcasted_iota(jnp.int32, (SEQ, 1), 0)
        live = (place >= PATCHES) & (place < PATCHES + lens[t * images + i])
        d = tgrad[rs, :]
        part = lax.dot_general(hots[i], d, NN, precision=lax.Precision.HIGHEST, preferred_element_type=F32)
        total = part if total is None else total + part
        tgrad[rs, :] = jnp.where(live, 0.0, d)
    pgrad[...] = total


def local_call(tok, table, lens, trows, g1, b1, qvb, ob, g2, b2, upb, db, cot, wqkv, wout, wup, wdn):
    rows = tok.shape[0]
    V = pl.BlockSpec(memory_space=pltpu.VMEM)
    S = pl.BlockSpec(memory_space=pltpu.SMEM)
    images = rows // SEQ
    return pl.pallas_call(
        functools.partial(compute, rows),
        out_shape=(jax.ShapeDtypeStruct((rows, D), BF), jax.ShapeDtypeStruct((rows, D), F32), jax.ShapeDtypeStruct((PROMPTS, D), F32)),
        in_specs=[S] + [V] * 16,
        out_specs=(V, V, V),
        scratch_shapes=[
            pltpu.VMEM((rows, D), F32),
            pltpu.VMEM((rows, D), BF),
            pltpu.VMEM((NZ, rows, 3 * QW), BF),
            pltpu.VMEM((NZ, images * HZ, SEQ, SEQ), BF),
            pltpu.VMEM((NZ, rows, QW), BF),
            pltpu.VMEM((rows, D), F32),
            pltpu.VMEM((rows, D), BF),
            pltpu.VMEM((rows, NZ * FZ), BF),
            pltpu.VMEM((rows, NZ * FZ), BF),
            pltpu.VMEM((rows, D), F32),
            pltpu.VMEM((rows, D), BF),
            pltpu.VMEM((NZ, rows, QW), BF),
            pltpu.VMEM((NZ, rows, 3 * QW), BF),
        ],
        compiler_params=pltpu.CompilerParams(vmem_limit_bytes=60 * 2**20),
    )(lens, tok, table, trows, g1, b1, qvb, ob, g2, b2, upb, db, cot, wqkv, wout, wup, wdn)


def body(tokens, prompt_table, lengths, table_rows, ln1_gain, ln1_bias, w_qkv, qv_bias, w_out, out_bias,
         ln2_gain, ln2_bias, w_up, up_bias, w_down, down_bias, cotangent):
    blk = jnp.concatenate([w_qkv[0], w_qkv[1], w_qkv[2], w_out.T, w_up, w_down.T], axis=1).astype(BF)
    g = lax.all_gather(blk, "dp", axis=0, tiled=True)
    g = lax.all_gather(g, "tensor", axis=0)
    wqkv, wout, wup, wdn = g[:, :, :576], g[:, :, 576:768], g[:, :, 768:1536], g[:, :, 1536:]
    bias = jnp.concatenate([qv_bias[0], jnp.zeros_like(qv_bias[0]), qv_bias[1], up_bias])
    bg = lax.all_gather(bias, "tensor", axis=0)
    qvb = bg[:, None, :576]
    upb = bg[:, None, 576:]
    o, tg, pg = local_call(tokens, prompt_table, lengths, table_rows, ln1_gain[None], ln1_bias[None], qvb, out_bias[None],
                           ln2_gain[None], ln2_bias[None], upb, down_bias[None], cotangent, wqkv, wout, wup, wdn)
    return o, tg, lax.psum(pg, ("dp", "tensor"))


def solution(mesh):
    row = P(("dp", "tensor"), None)
    return jax.shard_map(
        body, mesh=mesh,
        in_specs=(row, P(), P("dp"), P("dp", None), P(), P(), P(None, "dp", "tensor"), P(None, "tensor"), P("tensor", "dp"),
                  P(), P(), P(), P("dp", "tensor"), P("tensor"), P("tensor", "dp"), P(), row),
        out_specs=(row, row, P()), check_vma=False)
```

time: 832 us -> 443 us (0.53)
  waiting for transfers between devices: 584 us -> 300 us
  matrix products: 87.3 us -> 0 us
  Pallas kernels: 0 us -> 80.1 us
  blocking collectives: 53.4 us -> 13.4 us
  local copies, waits for them, and re-layouts: 59.9 us -> 30.5 us
  other arithmetic: 25.4 us -> 3.41 us
    reduce_scatter x4 -> x0, waiting for transfers between devices: 271 us -> none  [the longest x1 74.1 us: body(): lax.psum_scatter(jnp.einsum('rck,cdk->rd', d_qkv, qkv_w, preferred_elemen...]
    dot_general x37 -> x0, matrix products: 87.3 us -> none  [the longest x1 21.6 us: body(): jnp.dot(hidden, down_w, preferred_element_type=jnp.float32)]
    pallas_call x0 -> x1, Pallas kernels: none -> 80.1 us  [local_call(): pl.pallas_call(functools.partial(compute, rows), out_shape=(jax.ShapeDtyp...]
    all_gather x2 -> x0, blocking collectives: 53.4 us -> none  [the longest x1 27 us: body(): lax.all_gather(w_qkv.astype(jnp.bfloat16), 'dp', axis=1, tiled=True)]
    reshape x5 -> x0, local copies, waits for them, and re-layouts: 19.3 us -> none  [the longest x1 7.45 us: body(): packed = qkv_low.reshape(pair_count, 2, SEQ, 3, heads_here, HD)]
    slice x1 -> x5, local copies, waits for them, and re-layouts: 0.01 us -> 16.8 us  [the longest x1 7.97 us: body(): g[:, :, 1536:]]
    unnamed x0 -> x1, blocking collectives: none -> 13.4 us
    all_gather x6 -> x2, waiting for transfers between devices: 169 us -> 156 us  [the longest x1 106 us: body(): g = lax.all_gather(g, 'tensor', axis=0)]
  transfers between devices with their start and end apart: 11 -> 3, of which waited for: 9 -> 3; matrix products, arithmetic and copies ran while one was open for 5% -> 3% of each run, Pallas kernels for 0% -> 0%
where the time goes in v1:
time: 443 us; the launch traced here: 442 us
  waiting for transfers between devices  300 us (68%)
  Pallas kernels  80.1 us (18%)
  local copies, waits for them, and re-layouts  30.5 us (7%)
  between operations  14.4 us (3%)
  blocking collectives  13.4 us (3%)
    psum x1, waiting for transfers between devices, body(): return (o, tg, lax.psum(pg, ('dp', 'tensor')))  145 us
    all_gather x1, waiting for transfers between devices, body(): g = lax.all_gather(g, 'tensor', axis=0)  106 us
    pallas_call x1, Pallas kernels, local_call(): pl.pallas_call(functools.partial(compute, rows), out_shape=(jax.ShapeDtyp...  80.1 us
    all_gather x1, waiting for transfers between devices, body(): g = lax.all_gather(blk, 'dp', axis=0, tiled=True)  49.3 us
    unnamed x1, blocking collectives  13.4 us
  transfers between devices with their start and end apart: 3, of which 3 were waited for; matrix products, arithmetic and copies ran while one was open for 3% of the time, Pallas kernels for 0%

profile of v1, /device:TPU:1, one launch (start us, length us, event | category | flops | bytes accessed | tf_op | source)
XLA Modules:
  0.0 442.3 jit_solution(4252790943425881996)
XLA Ops:
  7.2 0.0 all-gather.5.cloned.1.call-start
  7.2 0.9 convert.22
  8.1 0.9 convert.24
  9.0 0.9 convert_bitcast_fusion
  9.9 0.7 convert_bitcast_fusion.1
  10.6 0.7 concatenate.8
  11.4 0.0 all-gather.5.cloned.1.call-update
  11.4 0.0 all-gather.7.cloned.1.call-start
  11.4 49.3 %all-gather.5.cloned.1.call-done = bf16[768,2304]{1,0:T(8,128)(2,1)} async-done(((bf16[24,2304]{1,0:T(8,128)(2,1)}), bf16[768,2304]{1,0:T(8,128)(2,1)}) %all-gather.5.cloned.1.call-update) | async-done | bytes 3538960 | tf_op jit(solution)/shard_map/all_gather | solution.py:245
  60.7 0.0 all-gather.7.cloned.1.call-update
  60.7 0.0 all-reduce.3.cloned.1.call-start
  60.8 1.2 dynamic-slice
  62.7 0.8 fusion.1
  63.4 0.8 concatenate.7
  64.2 0.3 dynamic-update-slice
  64.5 13.4 %all-reduce = f32[5376]{0:T(1024)S(1)} all-reduce(f32[5376]{0:T(1024)S(1)} %dynamic-update-slice), channel_id=2, replica_groups=mesh['dp'=32,'tensor'=4] {'tensor'}, use_global_device_ids=true, to_apply=%add | all-reduce | flops 5376 | bytes 43008
  77.9 0.1 reshape.6
  78.0 0.1 slice.48
  78.1 0.6 broadcast_in_dim.34.upb
  78.7 0.6 copy.20.qvb
  79.3 1.3 broadcast_in_dim.27.g1
  80.6 1.3 broadcast_in_dim.28.b1
  81.9 1.3 broadcast_in_dim.31.ob
  83.2 1.3 broadcast_in_dim.32.g2
  84.4 1.3 broadcast_in_dim.33.b2
  85.7 1.3 broadcast_in_dim.35.db
  87.0 106.4 %all-gather.7.cloned.1.call-done = bf16[3072,2304]{1,0:T(8,128)(2,1)} async-done(((bf16[768,2304]{1,0:T(8,128)(2,1)}), bf16[3072,2304]{1,0:T(8,128)(2,1)}) %all-gather.7.cloned.1.call-update) | async-done | bytes 14155792 | tf_op jit(solution)/shard_map/all_gather | solution.py:246
  193.4 8.0 %fusion = (bf16[4,768,768]{2,1,0:T(8,128)(2,1)}, bf16[4,768,768]{2,1,0:T(8,128)(2,1)}) fusion(bf16[4,768,2304]{2,1,0:T(8,128)(2,1)} %bitcast.16), kind=kLoop, calls=%fused_computation.6 | loop fusion | bytes 18874368 | tf_op jit(solution)/shard_map/slice | solution.py:247
  201.4 4.4 %slice.52.wqkv = bf16[4,768,576]{2,1,0:T(8,128)(2,1)} slice(bf16[4,768,2304]{2,1,0:T(8,128)(2,1)} %bitcast.17), slice={[0:4], [0:768], [0:576]} | slice | bytes 7077888 | tf_op jit(solution)/shard_map/slice | solution.py:247
  205.8 3.6 slice.53.wout
  209.4 80.1 %shard_map.184 = (bf16[608,768]{1,0:T(8,128)(2,1)}, f32[608,768]{1,0:T(8,128)}, f32[100,768]{1,0:T(8,128)}) custom-call(s32[8]{0:T(128)} %lens.1, bf16[608,768]{1,0:T(8,128)(2,1)} %tok.1, f32[100,768]{1,0:T(8,128)} %table.1, s32[8,100]{1,0:T(8,128)} %trows.1, f32[1,768]{1,0:T(1,128)} %broadcast_in_dim.27.g1, f32[1,768]{1,0:T(1,128)} %broadcast_in_dim.28.b1, ...), custom_call_target="tpu_custom_call" | custom-call | tf_op jit(solution)/shard_map/pallas_call | solution.py:218
  289.5 0.0 all-reduce.3.cloned.1.call-update
  289.5 144.5 %all-reduce.3.cloned.1.call-done = f32[100,768]{1,0:T(8,128)} async-done(((f32[100,768]{1,0:T(8,128)}), f32[100,768]{1,0:T(8,128)}) %all-reduce.3.cloned.1.call-update) | async-done | bytes 307216 | tf_op jit(solution)/shard_map/psum | solution.py:254
  434.1 1.7 copy.23
  (4 shorter events, 0.0 us)
Async XLA Ops:
  7.2 53.5 %all-gather.5.cloned.1.call-start = ((), (), s32[]{:S(2)}) async-start(), calls=%async_computation | async-start | bytes 3649536 | tf_op jit(solution)/shard_map/all_gather | solution.py:245
  11.4 182.0 %all-gather.7.cloned.1.call-start = ((), (), s32[]{:S(2)}) async-start(), calls=%async_computation.2 | async-start | bytes 17694720 | tf_op jit(solution)/shard_map/all_gather | solution.py:246
  60.7 373.3 %all-reduce.3.cloned.1.call-start = ((), (), s32[]{:S(2)}) async-start(), calls=%async_computation.1 | async-start | bytes 638976 | tf_op jit(solution)/shard_map/psum | solution.py:254
Sparse Core Ops, SparseCore 0:
  11.5 49.1 all-gather.4
  62.4 131.0 all-gather.6
  289.7 144.3 all-reduce.2

commit v2 on v1

--- a/solution.py
+++ b/solution.py
@@ -23,6 +23,8 @@
 NT = (((1,), (1,)), ((), ()))
 TN = (((0,), (0,)), ((), ()))
 CH = 32
+MESH = pl.DeviceIdType.MESH
+ORDERS = ((0, 1, 2), (1, 2, 0), (2, 0, 1))
 
 
 def mm(a, b, dims=NN):
@@ -51,10 +53,156 @@
     return r * (e - jnp.mean(e, axis=-1, keepdims=True) - n * jnp.mean(e * n, axis=-1, keepdims=True))
 
 
-def compute(rows, lens, tok, table, trows, g1, b1, qvb, ob, g2, b2, upb, db, cot,
-            wqkv, wout, wup, wdn, out, tgrad, pgrad,
-            inp, fin, qkv, probs, att, mid, sin, hid, dup, dmid, dml, dat, dqkv):
+class Gather:
+    def __init__(self, G, stage, other, psem, ssem, rsem, fsem, gsem):
+        dp = lax.axis_index("dp")
+        z = lax.axis_index("tensor")
+        self.core = lax.rem(dp, 2)
+        chip = lax.div(dp, 2)
+        self.at = (lax.rem(chip, 4), lax.div(chip, 4), z)
+        self.G, self.stage, self.other = G, stage, other
+        self.psem, self.ssem, self.rsem, self.fsem, self.gsem = psem, ssem, rsem, fsem, gsem
+
+    def device(self, at, core):
+        return ((at[1] * 4 + at[0]) * 2 + core, at[2])
+
+    def moved(self, axis, step):
+        at = list(self.at)
+        at[axis] = lax.rem(at[axis] + step, 4)
+        return tuple(at)
+
+    def barrier(self):
+        sem = pltpu.get_barrier_semaphore()
+        pl.semaphore_signal(sem, inc=1, device_id=self.device(self.at, 1 - self.core), device_id_type=MESH)
+        for d in (1, 2, 3):
+            pl.semaphore_signal(sem, inc=1, device_id=self.device(self.moved(2, d), self.core), device_id_type=MESH)
+        for i in range(1, 16):
+            pl.semaphore_signal(sem, inc=1, device_id=self.plane_peer(i), device_id_type=MESH)
+        pl.semaphore_wait(sem, 19)
+
+    def plane_peer(self, i):
+        chip = lax.rem(self.at[1] * 4 + self.at[0] + i, 16)
+        return (chip * 2 + self.core, self.at[2])
+
+    def bias_copy(self, bias, sems, d):
+        ref = bias.at[self.at[2]]
+        return pltpu.make_async_remote_copy(src_ref=ref, dst_ref=ref, send_sem=sems.at[0, d - 1], recv_sem=sems.at[1, d - 1],
+            device_id=self.device(self.moved(2, d), self.core), device_id_type=MESH)
+
+    def cols(self, core):
+        return pl.ds(pl.multiple_of(core * 384, 128), 384)
+
+    def pre(self, g):
+        return pltpu.make_async_remote_copy(
+            src_ref=self.stage.at[g], dst_ref=self.other.at[g], send_sem=self.psem.at[0, g], recv_sem=self.psem.at[1, g],
+            device_id=self.device(self.at, 1 - self.core), device_id_type=MESH)
+
+    def assemble(self, g):
+        c = self.cols(self.core)
+        mine, theirs = self.stage[g, :, c], self.other[g, :, c]
+        first = self.core == 0
+        both = jnp.concatenate([jnp.where(first, mine, theirs), jnp.where(first, theirs, mine)], axis=0).astype(BF)
+        x, y, z = self.at
+        for p in range(3):
+            self.G[g, z, y, x, p, :, c] = both[p * 16:(p + 1) * 16]
+
+    def view(self, g, p, phase, at, core):
+        order = ORDERS[p]
+        where = list(at)
+        for axis in order[:phase]:
+            where[axis] = slice(None)
+        return self.G.at[g, where[2], where[1], where[0], p, :, self.cols(core)]
+
+    def copy(self, g, p, phase, d):
+        axis = ORDERS[p][phase]
+        ref = self.view(g, p, phase, self.at, self.core)
+        i = p * 9 + phase * 3 + d - 1
+        return pltpu.make_async_remote_copy(
+            src_ref=ref, dst_ref=ref, send_sem=self.ssem.at[g, i], recv_sem=self.rsem.at[g, i],
+            device_id=self.device(self.moved(axis, d), self.core), device_id_type=MESH)
+
+    def start(self, g, phase):
+        for d in (1, 3, 2):
+            for p in range(3):
+                self.copy(g, p, phase, d).start()
+
+    def arrive(self, g, phase):
+        for d in (1, 3, 2):
+            for p in range(3):
+                self.copy(g, p, phase, d).wait_recv()
+
+    def sent(self, g):
+        for phase in range(3):
+            for d in (1, 2, 3):
+                for p in range(3):
+                    self.copy(g, p, phase, d).wait_send()
+
+    def pass_on(self, g, p, d):
+        at = self.moved(ORDERS[p][2], 4 - d)
+        ref = self.view(g, p, 2, at, self.core)
+        return pltpu.make_async_remote_copy(
+            src_ref=ref, dst_ref=ref, send_sem=self.fsem.at[g, p * 4 + d], recv_sem=self.gsem.at[g, p * 4 + d],
+            device_id=self.device(self.at, 1 - self.core), device_id_type=MESH)
+
+    def forward_own(self, g):
+        for p in range(3):
+            self.pass_on(g, p, 0).start()
+
+    def forward(self, g):
+        for d in (1, 3, 2):
+            for p in range(3):
+                self.copy(g, p, 2, d).wait_recv()
+                self.pass_on(g, p, d).start()
+
+    def finish(self, g):
+        for d in range(4):
+            for p in range(3):
+                self.pass_on(g, p, d).wait_recv()
+
+    def drain(self, g):
+        for d in range(4):
+            for p in range(3):
+                self.pass_on(g, p, d).wait_send()
+
+
+def compute(rows, lens, tok, table, trows, g1_, b1_, ob_, g2_, b2_, db_, cot, qvb, upb, wq, wo, wu, wd,
+            out, tgrad, pgrad,
+            inp, fin, qkv, probs, att, mid, sin, hid, dup, dmid, dml, dat, dqkv,
+            G, stage, other, psem, ssem, rsem, fsem, gsem, bias, bsem,
+            part, half, slots, zslots, final, rs_s, rs_r, zs, ag_s, ag_r, sb):
     t = lax.axis_index("tensor")
+    row = lambda ref: ref[...].reshape(1, D)
+    g1, b1, ob, g2, b2, db = (row(r) for r in (g1_, b1_, ob_, g2_, b2_, db_))
+    net = Gather(G, stage, other, psem, ssem, rsem, fsem, gsem)
+    stage[0] = jnp.concatenate([wq[0], wq[1], wq[2], wo[...]], axis=1)
+    stage[1] = wu[...]
+    stage[2] = wd[...]
+    bias[t] = jnp.concatenate([qvb[0:1, :], jnp.zeros((1, QW), F32), qvb[1:2, :], jnp.zeros((1, 64), F32), upb[...].reshape(1, FZ)], axis=1)
+    net.barrier()
+    for d in (1, 2, 3):
+        net.bias_copy(bias, bsem, d).start()
+    for g in range(3):
+        net.pre(g).start()
+    for g in range(3):
+        net.pre(g).wait_recv()
+        net.assemble(g)
+        net.start(g, 0)
+    for g in range(3):
+        net.arrive(g, 0)
+        net.start(g, 1)
+    for g in range(3):
+        net.arrive(g, 1)
+        net.start(g, 2)
+        net.forward_own(g)
+    for g in range(3):
+        net.forward(g)
+    for d in (1, 2, 3):
+        net.bias_copy(bias, bsem, d).wait()
+    for g in range(3):
+        net.finish(g)
+    load = lambda g, z: G[g, z].reshape(768, 768)
+    wqkv = lambda z: load(0, z)[:, :576]
+    wout = lambda z: load(0, z)[:, 576:]
     images = rows // SEQ
     hots = []
     for i in range(images):
@@ -76,12 +224,12 @@
     def _(c):
         sl = pl.ds(pl.multiple_of(c * CH, CH), CH)
         n, _ = stats(inp[sl, :])
-        fin[sl, :] = (n * g1[...] + b1[...]).astype(BF)
+        fin[sl, :] = (n * g1 + b1).astype(BF)
 
     @pl.loop(0, NZ)
     def _(z):
-        x = mm(fin[...], wqkv[z])
-        qkv[z] = (x + qvb[z]).astype(BF)
+        x = mm(fin[...], wqkv(z))
+        qkv[z] = (x + bias[z, :, 0:576]).astype(BF)
 
     @pl.loop(0, NZ)
     def _(z):
@@ -106,16 +254,16 @@
     @pl.loop(0, images)
     def _(i):
         rs = pl.ds(pl.multiple_of(i * SEQ, SEQ), SEQ)
-        acc = mm(att[0, rs, :], wout[0], NT)
+        acc = mm(att[0, rs, :], wout(0), NT)
         for z in range(1, NZ):
-            acc += mm(att[z, rs, :], wout[z], NT)
-        mid[rs, :] = inp[rs, :] + acc + ob[...]
+            acc += mm(att[z, rs, :], wout(z), NT)
+        mid[rs, :] = inp[rs, :] + acc + ob
 
     @pl.loop(0, rows // CH)
     def _(c):
         sl = pl.ds(pl.multiple_of(c * CH, CH), CH)
         n, _ = stats(mid[sl, :])
-        sin[sl, :] = (n * g2[...] + b2[...]).astype(BF)
+        sin[sl, :] = (n * g2 + b2).astype(BF)
 
     TF = 256
     NF = FZ // TF
@@ -127,8 +275,8 @@
         fo = pl.ds(pl.multiple_of(j * TF, TF), TF)
         for i in range(images):
             rs = pl.ds(i * SEQ, SEQ)
-            u = mm(sin[rs, :], wup[z, :, f]) + upb[z, :, f]
-            dh = mm(cot[rs, :], wdn[z, :, f])
+            u = mm(sin[rs, :], G[1, z, :, :, :, :, f].reshape(768, TF)) + bias[z, :, pl.ds(pl.multiple_of(640 + (j % NF) * TF, 128), TF)]
+            dh = mm(cot[rs, :], G[2, z, :, :, :, :, f].reshape(768, TF))
             a, b = gelu_pair(u)
             hid[rs, fo] = a.astype(BF)
             dup[rs, fo] = (dh * b).astype(BF)
@@ -136,43 +284,43 @@
     @pl.loop(0, images)
     def _(i):
         rs = pl.ds(pl.multiple_of(i * SEQ, SEQ), SEQ)
-        acc = mm(hid[rs, 0:FZ], wdn[0], NT)
+        acc = mm(hid[rs, 0:FZ], load(2, 0), NT)
         for z in range(1, NZ):
-            acc += mm(hid[rs, z * FZ:(z + 1) * FZ], wdn[z], NT)
-        out[rs, :] = (mid[rs, :] + acc + db[...]).astype(BF)
+            acc += mm(hid[rs, z * FZ:(z + 1) * FZ], load(2, z), NT)
+        out[rs, :] = (mid[rs, :] + acc + db).astype(BF)
 
     @pl.loop(0, images)
     def _(i):
         rs = pl.ds(pl.multiple_of(i * SEQ, SEQ), SEQ)
-        acc = mm(dup[rs, 0:FZ], wup[0], NT)
+        acc = mm(dup[rs, 0:FZ], load(1, 0), NT)
         for z in range(1, NZ):
-            acc += mm(dup[rs, z * FZ:(z + 1) * FZ], wup[z], NT)
+            acc += mm(dup[rs, z * FZ:(z + 1) * FZ], load(1, z), NT)
         dmid[rs, :] = acc
 
     @pl.loop(0, rows // CH)
     def _(c):
         sl = pl.ds(pl.multiple_of(c * CH, CH), CH)
         n, r = stats(mid[sl, :])
-        d = cot[sl, :].astype(F32) + norm_back(dmid[sl, :], n, r, g2[...])
+        d = cot[sl, :].astype(F32) + norm_back(dmid[sl, :], n, r, g2)
         dmid[sl, :] = d
         dml[sl, :] = d.astype(BF)
 
     @pl.loop(0, NZ)
     def _(z):
-        dat[z] = mm(dml[...], wout[z]).astype(BF)
+        dat[z] = mm(dml[...], wout(z)).astype(BF)
 
     @pl.loop(0, NZ)
     def _(z):
         for i in range(images):
             rs = pl.ds(i * SEQ, SEQ)
             blk = qkv[z, rs, :]
-            db_ = dat[z, rs, :]
+            dab = dat[z, rs, :]
             dq, dk, dv = [], [], []
             for h in range(HZ):
                 q = blk[:, h * HD:(h + 1) * HD]
                 k = blk[:, QW + h * HD:QW + (h + 1) * HD]
                 v = blk[:, 2 * QW + h * HD:2 * QW + (h + 1) * HD]
-                do = db_[:, h * HD:(h + 1) * HD]
+                do = dab[:, h * HD:(h + 1) * HD]
                 p = probs[z, i * HZ + h]
                 dp = mm(do, v, NT)
                 dv.append(mm(p, do, TN).astype(BF))
@@ -186,16 +334,16 @@
     @pl.loop(0, images)
     def _(i):
         rs = pl.ds(pl.multiple_of(i * SEQ, SEQ), SEQ)
-        acc = mm(dqkv[0, rs, :], wqkv[0], NT)
+        acc = mm(dqkv[0, rs, :], wqkv(0), NT)
         for z in range(1, NZ):
-            acc += mm(dqkv[z, rs, :], wqkv[z], NT)
+            acc += mm(dqkv[z, rs, :], wqkv(z), NT)
         tgrad[rs, :] = acc
 
     @pl.loop(0, rows // CH)
     def _(c):
         sl = pl.ds(pl.multiple_of(c * CH, CH), CH)
         n, r = stats(inp[sl, :])
-        d = dmid[sl, :] + norm_back(tgrad[sl, :], n, r, g1[...])
+        d = dmid[sl, :] + norm_back(tgrad[sl, :], n, r, g1)
         tgrad[sl, :] = d
 
     total = None
@@ -204,17 +352,70 @@
         place = lax.broadcasted_iota(jnp.int32, (SEQ, 1), 0)
         live = (place >= PATCHES) & (place < PATCHES + lens[t * images + i])
         d = tgrad[rs, :]
-        part = lax.dot_general(hots[i], d, NN, precision=lax.Precision.HIGHEST, preferred_element_type=F32)
-        total = part if total is None else total + part
+        piece = lax.dot_general(hots[i], d, NN, precision=lax.Precision.HIGHEST, preferred_element_type=F32)
+        total = piece if total is None else total + piece
         tgrad[rs, :] = jnp.where(live, 0.0, d)
-    pgrad[...] = total
-
-
-def local_call(tok, table, lens, trows, g1, b1, qvb, ob, g2, b2, upb, db, cot, wqkv, wout, wup, wdn):
-    rows = tok.shape[0]
+    part[...] = jnp.concatenate([total, jnp.zeros((128 - PROMPTS, D), F32)], axis=0)
+
+    core, chip = net.core, net.at[1] * 4 + net.at[0]
+    mine, theirs = net.cols(core), net.cols(1 - core)
+    swap = pltpu.make_async_remote_copy(src_ref=part.at[:, theirs], dst_ref=half, send_sem=sb.at[0], recv_sem=sb.at[1],
+                                        device_id=net.device(net.at, 1 - core), device_id_type=MESH)
+    swap.start()
+    swap.wait()
+    part[:, mine] = part[:, mine] + half[...]
+
+    def scatter(i):
+        dst = lax.rem(chip + i, 16)
+        return pltpu.make_async_remote_copy(src_ref=part.at[pl.ds(pl.multiple_of(dst * 8, 8), 8), mine], dst_ref=slots.at[i],
+                                            send_sem=rs_s.at[i], recv_sem=rs_r.at[i], device_id=net.plane_peer(i), device_id_type=MESH)
+    for i in range(1, 16):
+        scatter(i).start()
+    here = pl.ds(pl.multiple_of(chip * 8, 8), 8)
+    acc = part[here, mine]
+    for i in range(1, 16):
+        scatter(i).wait_recv()
+        acc = acc + slots[i]
+    zslots[t] = acc
+
+    def zcopy(d):
+        return pltpu.make_async_remote_copy(src_ref=zslots.at[t], dst_ref=zslots.at[t], send_sem=zs.at[0, d], recv_sem=zs.at[1, d],
+                                            device_id=net.device(net.moved(2, d), core), device_id_type=MESH)
+    for d in (1, 2, 3):
+        zcopy(d).start()
+    for d in (1, 2, 3):
+        zcopy(d).wait()
+    final[here, mine] = (zslots[0] + zslots[1]) + (zslots[2] + zslots[3])
+
+    def spread(i):
+        ref = final.at[here, mine]
+        return pltpu.make_async_remote_copy(src_ref=ref, dst_ref=ref, send_sem=ag_s.at[i], recv_sem=ag_r.at[i],
+                                            device_id=net.plane_peer(i), device_id_type=MESH)
+    for i in range(1, 16):
+        spread(i).start()
+    for i in range(1, 16):
+        spread(i).wait_recv()
+    last = pltpu.make_async_remote_copy(src_ref=final.at[:, mine], dst_ref=final.at[:, mine], send_sem=sb.at[2], recv_sem=sb.at[3],
+                                        device_id=net.device(net.at, 1 - core), device_id_type=MESH)
+    last.start()
+    last.wait()
+    pgrad[...] = final[0:PROMPTS, :]
+    for i in range(1, 16):
+        scatter(i).wait_send()
+        spread(i).wait_send()
+    for g in range(3):
+        net.sent(g)
+        net.drain(g)
+        net.pre(g).wait_send()
+
+
+def body(tokens, prompt_table, lengths, table_rows, ln1_gain, ln1_bias, w_qkv, qv_bias, w_out, out_bias,
+         ln2_gain, ln2_bias, w_up, up_bias, w_down, down_bias, cotangent):
+    rows = tokens.shape[0]
     V = pl.BlockSpec(memory_space=pltpu.VMEM)
     S = pl.BlockSpec(memory_space=pltpu.SMEM)
     images = rows // SEQ
+    DMA = pltpu.SemaphoreType.DMA
     return pl.pallas_call(
         functools.partial(compute, rows),
         out_shape=(jax.ShapeDtypeStruct((rows, D), BF), jax.ShapeDtypeStruct((rows, D), F32), jax.ShapeDtypeStruct((PROMPTS, D), F32)),
@@ -234,24 +435,17 @@
             pltpu.VMEM((rows, D), BF),
             pltpu.VMEM((NZ, rows, QW), BF),
             pltpu.VMEM((NZ, rows, 3 * QW), BF),
+            pltpu.VMEM((3, 4, 4, 4, 3, 16, 768), BF),
+            pltpu.VMEM((3, 24, 768), F32), pltpu.VMEM((3, 24, 768), F32),
+            DMA((2, 3)), DMA((3, 27)), DMA((3, 27)), DMA((3, 12)), DMA((3, 12)),
+            pltpu.VMEM((NZ, 1, 1408), F32), DMA((2, 3)),
+            pltpu.VMEM((128, D), F32), pltpu.VMEM((128, 384), F32), pltpu.VMEM((16, 8, 384), F32), pltpu.VMEM((4, 8, 384), F32),
+            pltpu.VMEM((128, D), F32),
+            DMA((16,)), DMA((16,)), DMA((2, 4)), DMA((16,)), DMA((16,)), DMA((4,)),
         ],
-        compiler_params=pltpu.CompilerParams(vmem_limit_bytes=60 * 2**20),
-    )(lens, tok, table, trows, g1, b1, qvb, ob, g2, b2, upb, db, cot, wqkv, wout, wup, wdn)
-
-
-def body(tokens, prompt_table, lengths, table_rows, ln1_gain, ln1_bias, w_qkv, qv_bias, w_out, out_bias,
-         ln2_gain, ln2_bias, w_up, up_bias, w_down, down_bias, cotangent):
-    blk = jnp.concatenate([w_qkv[0], w_qkv[1], w_qkv[2], w_out.T, w_up, w_down.T], axis=1).astype(BF)
-    g = lax.all_gather(blk, "dp", axis=0, tiled=True)
-    g = lax.all_gather(g, "tensor", axis=0)
-    wqkv, wout, wup, wdn = g[:, :, :576], g[:, :, 576:768], g[:, :, 768:1536], g[:, :, 1536:]
-    bias = jnp.concatenate([qv_bias[0], jnp.zeros_like(qv_bias[0]), qv_bias[1], up_bias])
-    bg = lax.all_gather(bias, "tensor", axis=0)
-    qvb = bg[:, None, :576]
-    upb = bg[:, None, 576:]
-    o, tg, pg = local_call(tokens, prompt_table, lengths, table_rows, ln1_gain[None], ln1_bias[None], qvb, out_bias[None],
-                           ln2_gain[None], ln2_bias[None], upb, down_bias[None], cotangent, wqkv, wout, wup, wdn)
-    return o, tg, lax.psum(pg, ("dp", "tensor"))
+        compiler_params=pltpu.CompilerParams(collective_id=1, has_side_effects=True, vmem_limit_bytes=62 * 2**20),
+    )(lengths, tokens, prompt_table, table_rows, ln1_gain, ln1_bias, out_bias, ln2_gain, ln2_bias, down_bias, cotangent,
+      qv_bias, up_bias, w_qkv, w_out.T, w_up, w_down.T)
 
 
 def solution(mesh):

time: 443 us -> 152 us (0.34)
  waiting for transfers between devices: 300 us -> 0 us
  Pallas kernels: 80.1 us -> 147 us
  local copies, waits for them, and re-layouts: 30.5 us -> 4.28 us
  between operations: 14.4 us -> 0.66 us
  blocking collectives: 13.4 us -> 0 us
    all_gather x2 -> x0, waiting for transfers between devices: 156 us -> none  [the longest x1 106 us: body(): g = lax.all_gather(g, 'tensor', axis=0)]
    psum x1 -> x0, waiting for transfers between devices: 145 us -> none  [body(): return (o, tg, lax.psum(pg, ('dp', 'tensor')))]
    pallas_call x1, Pallas kernels: 80.1 us -> 147 us  [body(): pl.pallas_call(functools.partial(compute, rows), out_shape=(jax.ShapeDtyp...]
    slice x5 -> x0, local copies, waits for them, and re-layouts: 16.8 us -> none  [the longest x1 7.97 us: body(): g[:, :, 1536:]]
    unnamed x1 -> x0, blocking collectives: 13.4 us -> none
    broadcast_in_dim x10 -> x0, local copies, waits for them, and re-layouts: 8.88 us -> none  [the longest x1 1.28 us: body(): ln1_bias[None]]
  transfers between devices with their start and end apart: 3 -> 0, of which waited for: 3 -> 0; matrix products, arithmetic and copies ran while one was open for 3% -> 0% of each run, Pallas kernels for 0% -> 0%
where the time goes in v2:
time: 152 us
  Pallas kernels  147 us (97%)
  local copies, waits for them, and re-layouts  4.28 us (3%)
    pallas_call x1, Pallas kernels, body(): pl.pallas_call(functools.partial(compute, rows), out_shape=(jax.ShapeDtyp...  147 us
    unnamed x7, local copies, waits for them, and re-layouts  4.28 us

profile of v2, /device:TPU:1, one launch (start us, length us, event | category | flops | bytes accessed | tf_op | source)
XLA Modules:
  0.0 152.3 jit_solution(18217154856238209201)
XLA Ops:
  0.6 147.3 %shard_map.184 = (bf16[608,768]{1,0:T(8,128)(2,1)}, f32[608,768]{1,0:T(8,128)}, f32[100,768]{1,0:T(8,128)}) custom-call(s32[8]{0:T(128)} %lens.1, bf16[608,768]{1,0:T(8,128)(2,1)} %tok.1, f32[100,768]{1,0:T(8,128)} %table.1, s32[8,100]{1,0:T(8,128)} %trows.1, f32[768]{0:T(1024)} %g1_.1, f32[768]{0:T(1024)} %b1_.1, f32[768]{0:T(1024)} %ob_.1, f32[768]{0:T(1024)} %g2_.1, ...), custom_call_target="tpu_custom_call" | custom-call | tf_op jit(solution)/shard_map/pallas_call | solution.py:419
  148.0 0.0 copy-start
  148.0 2.3 %copy.23 = bf16[608,768]{1,0:T(8,128)(2,1)} copy(bf16[608,768]{1,0:T(8,128)(2,1)} %get-tuple-element.6) | data formatting | bytes 1867776
  150.3 0.0 copy-done
  150.3 0.0 copy-start.1
  150.3 1.2 copy.24
  151.6 0.0 copy-done.1
  151.6 0.7 copy.25
Async XLA Ops:
  148.0 2.3 %copy-start = (f32[608,768]{1,0:T(8,128)S(1)}, f32[608,768]{1,0:T(8,128)}, u32[]{:S(2)}) copy-start(f32[608,768]{1,0:T(8,128)} %get-tuple-element.7) | copy-start | bytes 5603332
  150.3 1.2 copy-start.1
